TPU v7x, 512 devices: a whole 4x8x8 slice. The times are simulated.
512 devices in a mesh: patch: 64 (over y_lo, z, core), tensor: 8 (over x, y_hi).
Axes of the slice: x: 4, y: 8 (y_hi: 2, y_lo: 4; y = y_hi * 4 + y_lo), z: 8, core: 2. Of those that a mesh axis runs over, the one named last changes fastest.
Arguments:
- hidden_in: bfloat16 [8192, 5120], P('patch', 'tensor'), may hold values from -6 to 6
- queries: bfloat16 [8192, 3072], P('patch', 'tensor'), may hold values from -16 to 16
- fresh_keys: bfloat16 [8192, 3072], P('patch', 'tensor'), may hold values from -6 to 6
- fresh_values: bfloat16 [8192, 3072], P('patch', 'tensor'), may hold values from -6 to 6
- stale_keys: bfloat16 [8192, 3072], P('patch', 'tensor'), may hold values from -8 to 8
- stale_values: bfloat16 [8192, 3072], P('patch', 'tensor'), may hold values from -6 to 6
- out_weight: bfloat16 [3072, 5120], P('tensor'), may hold values from -0.5 to 0.5
- gate: float32 [5120], P('tensor'), may hold values from 0.5 to 1.5
Outputs:
- mixed: bfloat16 [8192, 5120], P('patch', 'tensor')
All inputs are finite; a program needn't handle non-finite values.
Results may differ from a plain program's by a relative error of at most 0.017.
Values may be sent and summed in bfloat16 or wider, within the bound.
A program may use at most 64 MiB of HBM per device.

v0:
```python
import jax
import jax.numpy as jnp
from jax import lax
from jax.sharding import PartitionSpec as P

HEAD_DIM = 128


def head_columns(matrix, head):
    return lax.dynamic_slice_in_dim(matrix, head * HEAD_DIM, HEAD_DIM, 1)


def head_scores(query_cols, key_cols, score_scale):
    return (
        lax.dot_general(
            query_cols, key_cols, (((1,), (1,)), ((), ())), preferred_element_type=jnp.float32
        )
        * score_scale
    )


def local(hidden_in, queries, fresh_keys, fresh_values, stale_keys, stale_values, out_weight, gate):
    tok_rows = queries.shape[0]
    col_width = queries.shape[1]
    heads_here = col_width // HEAD_DIM
    score_scale = HEAD_DIM ** (-0.5)
    own_block = lax.axis_index("patch")
    all_keys, all_values = (
        lax.all_gather(stale_keys, "patch", axis=0, tiled=True),
        lax.all_gather(stale_values, "patch", axis=0, tiled=True),
    )
    first_row = own_block * tok_rows
    all_keys = lax.dynamic_update_slice_in_dim(all_keys, fresh_keys, first_row, 0)
    all_values = lax.dynamic_update_slice_in_dim(all_values, fresh_values, first_row, 0)

    def whole_head(head):
        scores = head_scores(head_columns(queries, head), head_columns(all_keys, head), score_scale)
        row_max = jnp.max(scores, axis=-1, keepdims=True)
        weights = jnp.exp(scores - row_max)
        denominator = jnp.sum(weights, axis=-1, keepdims=True)
        summed = jnp.dot(
            weights.astype(jnp.bfloat16),
            head_columns(all_values, head),
            preferred_element_type=jnp.float32,
        )
        return summed / denominator

    attended = lax.map(whole_head, jnp.arange(heads_here, dtype=jnp.int32))
    attended = attended.transpose(1, 0, 2).reshape(tok_rows, col_width).astype(jnp.bfloat16)
    partial_value = jnp.dot(attended, out_weight, preferred_element_type=jnp.float32)
    projected = lax.psum_scatter(
        partial_value.astype(jnp.bfloat16), "tensor", scatter_dimension=1, tiled=True
    ).astype(jnp.float32)
    mixed = hidden_in.astype(jnp.float32) + gate[None, :] * projected
    return mixed.astype(jnp.bfloat16)


def solution(mesh):
    return jax.shard_map(
        local,
        mesh=mesh,
        in_specs=(
            P("patch", "tensor"),
            P("patch", "tensor"),
            P("patch", "tensor"),
            P("patch", "tensor"),
            P("patch", "tensor"),
            P("patch", "tensor"),
            P("tensor", None),
            P("tensor"),
        ),
        out_specs=P("patch", "tensor"),
        check_vma=False,
    )
```

profile of v0, /device:TPU:56, one launch (start us, length us, event | category | flops | bytes accessed | tf_op | source)
XLA Modules:
  0.0 382.6 jit_solution(14620739404573818136)
XLA Ops:
  6.5 0.0 all-gather.5.cloned.1.call-start
  6.5 0.7 all-gather.5.cloned.1.call-update
  7.3 0.0 all-gather.3.cloned.1.call-start
  7.3 0.7 all-gather.3.cloned.1.call-update
  8.0 0.0 reduce-scatter.4.cloned.1.call-start
  8.1 128.8 %all-gather.5.cloned.1.call-done = bf16[8192,384]{1,0:T(8,128)(2,1)} async-done(((bf16[128,384]{1,0:T(8,128)(2,1)}), bf16[8192,384]{1,0:T(8,128)(2,1)}) %all-gather.5.cloned.1.call-update) | async-done | bytes 6291472 | tf_op jit(solution)/shard_map/all_gather | solution.py:30
  136.8 1.5 constant_dynamic-update-slice_fusion.1
  138.4 121.4 %all-gather.3.cloned.1.call-done = bf16[8192,384]{1,0:T(8,128)(2,1)} async-done(((bf16[128,384]{1,0:T(8,128)(2,1)}), bf16[8192,384]{1,0:T(8,128)(2,1)}) %all-gather.3.cloned.1.call-update) | async-done | bytes 6291472 | tf_op jit(solution)/shard_map/all_gather | solution.py:29
  259.8 1.5 constant_dynamic-update-slice_fusion.2
  261.3 21.1 %while.10 = (s32[]{:T(128)}, bf16[3,128,128]{1,2,0:T(8,128)(2,1)S(1)}, s32[3]{0:T(128)S(1)}, bf16[128,384]{1,0:T(8,128)(2,1)}, bf16[8192,384]{1,0:T(8,128)(2,1)}...) while((s32[]{:T(128)}, bf16[3,128,128]{1,2,0:T(8,128)(2,1)S(1)}, ...), condition=%wide.region_3.4_spmd, body=%wide.region_0.3_spmd.sunk | while | flops 543194880 | bytes 16977576 | solution.py:48
  261.3 0.6 dynamic_slice.34
  262.6 2.4 fusion.30
  265.0 0.8 fusion.31
  265.7 2.5 fusion.32
  268.2 0.1 copy.16
  268.4 0.6 dynamic_slice.34
  269.6 2.4 fusion.30
  272.0 0.8 fusion.31
  272.8 2.5 fusion.32
  275.3 0.1 copy.16
  275.4 0.6 dynamic_slice.34
  276.6 2.4 fusion.30
  279.0 0.8 fusion.31
  279.8 2.5 fusion.32
  282.3 0.1 copy.16
  282.4 0.0 copy-start
  282.4 0.0 copy-start.1
  282.5 3.0 convolution_convert_fusion
  285.5 1.4 copy.11
  286.9 0.0 reduce-scatter.4.cloned.1.call-update
  287.0 87.3 %reduce-scatter.4.cloned.1.call-done = bf16[640,128]{1,0:T(8,128)(2,1)} async-done(((bf16[5120,128]{1,0:T(8,128)(2,1)}), bf16[640,128]{1,0:T(8,128)(2,1)}) %reduce-scatter.4.cloned.1.call-update) | async-done | bytes 163856
  374.2 1.1 copy.12
  375.3 0.0 copy-done
  375.3 0.0 copy-done.1
  375.3 0.7 add_convert_fusion
  (5 shorter events, 0.0 us)
Async XLA Ops:
  6.5 130.3 %all-gather.5.cloned.1.call-start = ((), (), s32[]{:S(2)}) async-start(), calls=%async_computation.2 | async-start | bytes 6389760 | tf_op jit(solution)/shard_map/all_gather | solution.py:30
  7.3 252.5 %all-gather.3.cloned.1.call-start = ((), (), s32[]{:S(2)}) async-start(), calls=%async_computation.1 | async-start | bytes 6389760 | tf_op jit(solution)/shard_map/all_gather | solution.py:29
  8.0 366.2 %reduce-scatter.4.cloned.1.call-start = ((), (), s32[]{:S(2)}) async-start(), calls=%async_computation.3 | async-start | bytes 1474560
  282.4 92.9 %copy-start = (bf16[128,640]{1,0:T(8,128)(2,1)S(1)}, bf16[128,640]{1,0:T(8,128)(2,1)}, u32[]{:S(2)}) copy-start(bf16[128,640]{1,0:T(8,128)(2,1)} %param.10) | copy-start | bytes 491524
  282.4 92.9 %copy-start.1 = (f32[640]{0:T(1024)S(1)}, f32[640]{0:T(1024)}, u32[]{:S(2)}) copy-start(f32[640]{0:T(1024)} %param.17) | copy-start | bytes 7684
Sparse Core Ops, SparseCore 0:
  9.5 127.2 all-gather.4
  139.0 120.7 all-gather.2
  287.1 87.1 reduce-scatter.3
where the time goes:
time: 387 us; the launch traced here: 383 us
  waiting for transfers between devices  339 us (88%)
  matrix products  17.7 us (5%)
  between operations  13.2 us (3%)
  local copies, waits for them, and re-layouts  7.77 us (2%)
    all_gather x1, waiting for transfers between devices, local(): lax.all_gather(stale_values, 'patch', axis=0, tiled=True)  129 us
    all_gather x1, waiting for transfers between devices, local(): lax.all_gather(stale_keys, 'patch', axis=0, tiled=True)  121 us
    unnamed x4, waiting for transfers between devices  88.7 us
  transfers between devices with their start and end apart: 3, of which 3 were waited for; matrix products, arithmetic and copies ran while one was open for 0% of the time, Pallas kernels for 0%

commit v1 on v0

v1 whole, which is shorter than its diff:
```python
import functools

import jax
import jax.numpy as jnp
from jax import lax
from jax.experimental import pallas as pl
from jax.experimental.pallas import tpu as pltpu
from jax.sharding import PartitionSpec as P

HEAD_DIM = 128
HEADS = 3
TOK = 128
COLS = 640
NY, NZ, NX = 4, 8, 4
SCALE = 1.4426950408889634 * HEAD_DIM**-0.5
MESH = pl.DeviceIdType.MESH
F32, BF16 = jnp.float32, jnp.bfloat16

ORDER = (
    (0, 1), (1, 1), (0, 2), (2, 1), (0, 3), (1, 2),
    (0, 4), (2, 2), (1, 3), (2, 3), (1, 4), (2, 4),
)


def flip(i, k):
    if k == 1:
        return i + 1 - 2 * (i % 2)
    if k == 2:
        return i + 2 - 4 * (i // 2)
    return 3 - i


def dot_t(a, b):
    return lax.dot_general(a, b, (((1,), (1,)), ((), ())), preferred_element_type=F32)


def dot(a, b):
    return jnp.dot(a, b, preferred_element_type=F32)


def kernel(
    hid, q, fk, fv, sk, sv, w, gate, out,
    kv, qb, m, l, acc, osend, orecv, att, attx, wb, pacc, ysend, yrecv, hidv, gatev,
    loc_sem, w_loc, z_send, z_recv, c_send, c_recv, q_send, q_recv, o_send, o_recv,
    a_send, a_recv, wx_send, wx_recv, wc_send, wc_recv, y_send, y_recv,
):
    p, t = lax.axis_index("patch"), lax.axis_index("tensor")
    y, z, c = p // (2 * NZ), (p // 2) % NZ, p % 2
    x, yh = t // 2, t % 2

    def dev(y, z, c, x, yh):
        return ((y * NZ + z) * 2 + c, x * 2 + yh)

    zp, zm = dev(y, (z + 1) % NZ, c, x, yh), dev(y, (z + NZ - 1) % NZ, c, x, yh)
    sib = dev(y, z, 1 - c, x, yh)
    ys = [None] + [dev(flip(y, k), z, c, x, yh) for k in (1, 2, 3)]
    xs = [None] + [dev(y, z, c, flip(x, k), yh) for k in (1, 2, 3)]
    mate = dev(y, z, c, x, 1 - yh)

    sent = []

    def rc(src, dst, ssem, rsem, to):
        return pltpu.make_async_remote_copy(
            src_ref=src, dst_ref=dst, send_sem=ssem, recv_sem=rsem,
            device_id=to, device_id_type=MESH,
        )

    def push(src, dst, ssem, rsem, to):
        copy = rc(src, dst, ssem, rsem, to)
        copy.start()
        sent.append(copy)

    def got(dst, ssem, rsem):
        rc(dst, dst, ssem, rsem, sib).wait_recv()

    def cols(h):
        return pl.ds(h * HEAD_DIM, HEAD_DIM)

    first, later = [], []
    for h in range(HEADS):
        for n, (src, dst) in enumerate((
            (sk.at[:, cols(h)], kv.at[h, 0, 0, 0]),
            (sv.at[:, cols(h)], kv.at[h, 0, 1, 0]),
            (q.at[:, cols(h)], qb.at[h, 0]),
        )):
            first.append(pltpu.make_async_copy(src, dst, loc_sem.at[h, n]))
    for h in range(HEADS):
        for n, (src, dst) in enumerate((
            (fk.at[:, cols(h)], kv.at[h, 0, 0, 2]),
            (fv.at[:, cols(h)], kv.at[h, 0, 1, 2]),
        )):
            later.append(pltpu.make_async_copy(src, dst, loc_sem.at[h, 3 + n]))
    own_cols = pl.ds(pl.multiple_of((2 * x + yh) * COLS, 128), COLS)
    mate_cols = pl.ds(pl.multiple_of((2 * x + 1 - yh) * COLS, 128), COLS)
    later.append(pltpu.make_async_copy(hid, hidv, loc_sem.at[0, 5]))
    later.append(pltpu.make_async_copy(gate, gatev, loc_sem.at[1, 5]))
    w_own = [
        pltpu.make_async_copy(w.at[:, :, own_cols], wb.at[0, :, 0], w_loc.at[0]),
        pltpu.make_async_copy(w.at[:, :, mate_cols], wb.at[1, :, 0], w_loc.at[1]),
    ]
    for copy in first:
        copy.start()

    barrier = pltpu.get_barrier_semaphore()
    peers = [zp, zm, sib, *ys[1:], *xs[1:], mate]
    for peer in peers:
        pl.semaphore_signal(barrier, inc=1, device_id=peer, device_id_type=MESH)
    for copy in first:
        copy.wait()
    pl.semaphore_wait(barrier, len(peers))

    def z_refs(h, d):
        if d < 4:
            return kv.at[h, d, :, 0], kv.at[h, d, :, 1]
        return kv.at[h, 4, 0, 0], kv.at[h, 4, 1, 0]

    def z_start(h, d):
        if d == 1:
            src = kv.at[h, 0, :, 0], kv.at[h, 0, :, 0]
        elif d < 4:
            src = kv.at[h, d - 1, :, 0], kv.at[h, d - 1, :, 1]
        else:
            src = kv.at[h, 3, 0, 0], kv.at[h, 3, 1, 1]
        dst = z_refs(h, d)
        for way, to in ((0, zp), (1, zm)):
            push(src[way], dst[way], z_send.at[way, h, d - 1], z_recv.at[way, h, d - 1], to)

    def c_refs(h, d):
        if d in (0, 4):
            return kv.at[h, d, :, 0], kv.at[h, d, :, 1]
        return kv.at[h, d, :, pl.ds(0, 2)], kv.at[h, d, :, pl.ds(2, 2)]

    def c_start(h, d):
        src, dst = c_refs(h, d)
        push(src, dst, c_send.at[h, d], c_recv.at[h, d], sib)

    def relay(h, d):
        dst = z_refs(h, d)
        for way in (0, 1):
            got(dst[way], z_send.at[way, h, d - 1], z_recv.at[way, h, d - 1])
        if d < 4:
            z_start(h, d + 1)
        c_start(h, d)

    def q_start(h):
        for k in (1, 2, 3):
            push(qb.at[h, 0], qb.at[h, k], q_send.at[h, k - 1], q_recv.at[h, k - 1], ys[k])

    def w_start(h):
        for k in (1, 2, 3):
            there = flip(x, k)
            half = (yh + c) % 2
            at = pl.ds(pl.multiple_of((2 * there + half) * COLS, 128), COLS)
            push(w.at[h, :, at], wb.at[c, h, k], wx_send.at[h, k - 1], wx_recv.at[h, k - 1], xs[k])

    def w_relay(h):
        for k in (1, 2, 3):
            got(wb.at[c, h, k], wx_send.at[h, k - 1], wx_recv.at[h, k - 1])
            push(wb.at[c, h, k], wb.at[c, h, k], wc_send.at[h, k - 1], wc_recv.at[h, k - 1], sib)

    def attend(h, rows, count, keys, values, fresh_start):
        qv = qb[h, pl.ds(rows, count)].reshape(count * TOK, HEAD_DIM)
        at = pl.ds(rows * TOK, count * TOK)
        s = dot_t(qv, keys) * SCALE
        top = jnp.max(s, axis=-1, keepdims=True)
        n = s.shape[1] // 128
        if fresh_start:
            m_new = jnp.broadcast_to(top, (count * TOK, 128))
        else:
            m_old = m[h, at, :]
            m_new = jnp.maximum(m_old, top)
            alpha = jnp.exp2(m_old - m_new)
        parts = [jnp.exp2(s[:, j * 128 : (j + 1) * 128] - m_new) for j in range(n)]
        total = functools.reduce(jnp.add, parts)
        pv = dot(jnp.concatenate([e.astype(BF16) for e in parts], axis=1), values)
        m[h, at, :] = m_new
        if fresh_start:
            l[h, at, :] = total
            acc[h, at, :] = pv
        else:
            l[h, at, :] = alpha * l[h, at, :] + total
            acc[h, at, :] = alpha * acc[h, at, :] + pv

    def work(h, d):
        src, dst = c_refs(h, d)
        got(dst, c_send.at[h, d], c_recv.at[h, d])
        if d == 0:
            for k in (1, 2, 3):
                got(qb.at[h, k], q_send.at[h, k - 1], q_recv.at[h, k - 1])
            both = kv[h, 0, :, pl.ds(1, 2)]
            attend(h, 0, 1, both[0].reshape(-1, 128), both[1].reshape(-1, 128), True)
            both = kv[h, 0, :, pl.ds(0, 2)]
            attend(h, 1, 3, both[0].reshape(-1, 128), both[1].reshape(-1, 128), True)
        else:
            n = 2 if d == 4 else 4
            keys = kv[h, d, 0, pl.ds(0, n)].reshape(n * TOK, 128)
            values = kv[h, d, 1, pl.ds(0, n)].reshape(n * TOK, 128)
            for r in (0, 2):
                attend(h, r, 2, keys, values, False)

    def finish(h):
        for k in (1, 2, 3, 0):
            at = pl.ds(k * TOK, TOK)
            total = jnp.sum(l[h, at, :], axis=-1, keepdims=True)
            o = acc[h, at, :] * (1.0 / total)
            lse = m[h, at, :] + jnp.log2(total)
            if k == 0:
                acc[h, at, :] = o
                m[h, at, :] = lse
                continue
            osend[h, k - 1, pl.ds(0, TOK), :] = o.astype(BF16)
            flat = lse.T[:16, :]
            hi = flat.astype(BF16)
            rest = flat - hi.astype(F32)
            mid = rest.astype(BF16)
            low = (rest - mid.astype(F32)).astype(BF16)
            row = lax.broadcasted_iota(jnp.int32, (16, 128), 0)
            three = jnp.where(
                row == 0, hi.astype(F32), jnp.where(row == 1, mid.astype(F32), low.astype(F32))
            )
            osend[h, k - 1, pl.ds(TOK, 16), :] = three.astype(BF16)
            push(
                osend.at[h, k - 1], orecv.at[h, k - 1],
                o_send.at[h, k - 1], o_recv.at[h, k - 1], ys[k],
            )

    def merge(h):
        own = pl.ds(0, TOK)
        os, lses = [acc[h, own, :]], [m[h, own, :]]
        for k in (1, 2, 3):
            got(orecv.at[h, k - 1], o_send.at[h, k - 1], o_recv.at[h, k - 1])
            os.append(orecv[h, k - 1, pl.ds(0, TOK), :].astype(F32))
            three = orecv[h, k - 1, pl.ds(TOK, 16), :].astype(F32)
            flat = three[0:1] + three[1:2] + three[2:3]
            lses.append(jnp.broadcast_to(flat, (TOK, 128)).T)
        top = functools.reduce(jnp.maximum, lses)
        ws = [jnp.exp2(e - top) for e in lses]
        den = functools.reduce(jnp.add, ws)
        num = functools.reduce(jnp.add, [a * b for a, b in zip(ws, os, strict=True)])
        result = (num / den).astype(BF16)
        att[h] = result
        attx[h, :, pl.ds(0, 128)] = result
        for k in (1, 2, 3):
            push(
                att.at[h], attx.at[h, :, pl.ds(k * 128, 128)],
                a_send.at[h, k - 1], a_recv.at[h, k - 1], xs[k],
            )

    def project(h):
        for k in (1, 2, 3):
            got(attx.at[h, :, pl.ds(k * 128, 128)], a_send.at[h, k - 1], a_recv.at[h, k - 1])
            got(wb.at[1 - c, h, k], wc_send.at[h, k - 1], wc_recv.at[h, k - 1])
        a = attx[h]
        for part in (1, 0):
            term = dot(a, wb[part, h].reshape(NX * TOK, COLS))
            if h > 0:
                term = pacc[part] + term
            if h < HEADS - 1 or part == 0:
                pacc[part] = term
            else:
                ysend[...] = term.astype(BF16)
                push(ysend, yrecv, y_send, y_recv, mate)

    z_start(0, 1)
    q_start(0)
    z_start(1, 1)
    for h in range(HEADS):
        c_start(h, 0)
    q_start(1)
    z_start(2, 1)
    q_start(2)
    for copy in later:
        copy.start()
    for h in range(HEADS):
        w_start(h)
    for copy in w_own:
        copy.start()
    for copy in later:
        copy.wait()

    todo = {i: [] for i in range(len(ORDER) + 1)}
    todo[1].append((0, 0))
    todo[2].append((0, 1))
    todo[3].append((1, 0))
    todo[4].append((1, 1))
    todo[5].append((0, 2))
    todo[6].append((2, 0))
    todo[7].append((0, 3))
    todo[7].append((2, 1))
    todo[8].append((0, 4))
    todo[8].append((1, 2))
    todo[9].append((2, 2))
    todo[10].append((1, 3))
    todo[11].append((2, 3))
    todo[11].append((1, 4))
    todo[12].append((2, 4))
    for i in range(len(ORDER) + 1):
        if i < len(ORDER):
            relay(*ORDER[i])
        for h, d in todo[i]:
            work(h, d)
            if d == 4:
                finish(h)
        if i == 9:
            w_relay(0)
        if i == 11:
            merge(0)
    w_relay(1)
    merge(1)
    for copy in w_own:
        copy.wait()
    project(0)
    merge(2)
    w_relay(2)
    project(1)
    project(2)
    got(yrecv, y_send, y_recv)
    projected = pacc[0] + yrecv[...].astype(F32)
    mixed = hidv[...].astype(F32) + gatev[...] * projected
    out[...] = mixed.astype(BF16)
    for copy in sent:
        copy.wait_send()


def local(hidden_in, queries, fresh_keys, fresh_values, stale_keys, stale_values, out_weight, gate):
    anywhere = pl.BlockSpec(memory_space=pl.ANY)
    vmem, dma = pltpu.VMEM, pltpu.SemaphoreType.DMA
    wide = (HEADS, NY * TOK, 128)
    return pl.pallas_call(
        kernel,
        out_shape=jax.ShapeDtypeStruct((TOK, COLS), BF16),
        in_specs=[anywhere] * 8,
        out_specs=pl.BlockSpec(memory_space=pltpu.VMEM),
        scratch_shapes=[
            vmem((HEADS, 5, 2, 4, TOK, 128), BF16),
            vmem((HEADS, NY, TOK, 128), BF16),
            vmem(wide, F32),
            vmem(wide, F32),
            vmem(wide, F32),
            vmem((HEADS, 3, TOK + 16, 128), BF16),
            vmem((HEADS, 3, TOK + 16, 128), BF16),
            vmem((HEADS, TOK, 128), BF16),
            vmem((HEADS, TOK, NX * 128), BF16),
            vmem((2, HEADS, NX, TOK, COLS), BF16),
            vmem((2, TOK, COLS), F32),
            vmem((TOK, COLS), BF16),
            vmem((TOK, COLS), BF16),
            vmem((TOK, COLS), BF16),
            vmem((1, COLS), F32),
            dma((HEADS, 6)),
            dma((2,)),
            dma((2, HEADS, 4)),
            dma((2, HEADS, 4)),
            dma((HEADS, 5)),
            dma((HEADS, 5)),
            *[dma((HEADS, 3)) for _ in range(10)],
            dma(()),
            dma(()),
        ],
        compiler_params=pltpu.CompilerParams(
            collective_id=0, has_side_effects=True, vmem_limit_bytes=40 * 2**20
        ),
    )(
        hidden_in, queries, fresh_keys, fresh_values, stale_keys, stale_values,
        out_weight.reshape(HEADS, TOK, -1), gate.reshape(1, COLS),
    )


def solution(mesh):
    split = P("patch", "tensor")
    return jax.shard_map(
        local,
        mesh=mesh,
        in_specs=(split,) * 6 + (P("tensor", None), P("tensor")),
        out_specs=split,
        check_vma=False,
    )
```

time: 387 us -> 69.3 us (0.18); the launches traced: 383 us -> 69 us
  waiting for transfers between devices: 339 us -> 0 us
  Pallas kernels: 0 us -> 60.1 us
  matrix products: 17.7 us -> 0 us
  between operations: 13.2 us -> 0.02 us
    all_gather x2 -> x0, waiting for transfers between devices: 250 us -> none  [the longest x1 129 us: local(): lax.all_gather(stale_values, 'patch', axis=0, tiled=True)]
    unnamed x4 -> x0, waiting for transfers between devices: 88.7 us -> none
    pallas_call x0 -> x1, Pallas kernels: none -> 60.1 us  [local(): pl.pallas_call(kernel, out_shape=jax.ShapeDtypeStruct((TOK, COLS), BF16),...]
    dot_general x7 -> x0, matrix products: 17.7 us -> none  [the longest x3 7.44 us: whole_head(): jnp.dot(weights.astype(jnp.bfloat16), head_columns(all_values, head), pre...]
    unnamed x6 -> x15, local copies, waits for them, and re-layouts: 2.52 us -> 8.16 us
  transfers between devices with their start and end apart: 3 -> 0, of which waited for: 3 -> 0; matrix products, arithmetic and copies ran while one was open for 0% -> 0% of each run, Pallas kernels for 0% -> 0%
where the time goes in v1:
time: 69.3 us; the launch traced here: 69 us
  Pallas kernels  60.1 us (87%)
  local copies, waits for them, and re-layouts  8.85 us (13%)
    pallas_call x1, Pallas kernels, local(): pl.pallas_call(kernel, out_shape=jax.ShapeDtypeStruct((TOK, COLS), BF16),...  60.1 us
    unnamed x15, local copies, waits for them, and re-layouts  8.16 us

profile of v1, /device:TPU:56, one launch (start us, length us, event | category | flops | bytes accessed | tf_op | source)
XLA Modules:
  0.0 69.0 jit_solution(3092056661972365211)
XLA Ops:
  0.0 0.7 reshape.7.gate
  0.7 0.0 copy-start
  0.7 2.1 %copy-done = bf16[384,5120]{1,0:T(8,128)(2,1)S(1)} copy-done((bf16[384,5120]{1,0:T(8,128)(2,1)S(1)}, bf16[384,5120]{1,0:T(8,128)(2,1)}, u32[]{:S(2)}) %copy-start) | copy-done | bytes 3932184
  2.8 0.0 copy-start.1
  2.8 0.9 %copy-done.1 = bf16[128,640]{1,0:T(8,128)(2,1)S(1)} copy-done((bf16[128,640]{1,0:T(8,128)(2,1)S(1)}, bf16[128,640]{1,0:T(8,128)(2,1)}, u32[]{:S(2)}) %copy-start.1) | copy-done | bytes 163864
  3.7 0.0 copy-start.2
  3.7 0.9 %copy-done.2 = bf16[128,384]{1,0:T(8,128)(2,1)S(1)} copy-done((bf16[128,384]{1,0:T(8,128)(2,1)S(1)}, bf16[128,384]{1,0:T(8,128)(2,1)}, u32[]{:S(2)}) %copy-start.2) | copy-done | bytes 98328
  4.6 0.0 copy-start.3
  4.6 0.9 %copy-done.3 = bf16[128,384]{1,0:T(8,128)(2,1)S(1)} copy-done((bf16[128,384]{1,0:T(8,128)(2,1)S(1)}, bf16[128,384]{1,0:T(8,128)(2,1)}, u32[]{:S(2)}) %copy-start.3) | copy-done | bytes 98328
  5.5 0.0 copy-start.4
  5.5 0.9 %copy-done.4 = bf16[128,384]{1,0:T(8,128)(2,1)S(1)} copy-done((bf16[128,384]{1,0:T(8,128)(2,1)S(1)}, bf16[128,384]{1,0:T(8,128)(2,1)}, u32[]{:S(2)}) %copy-start.4) | copy-done | bytes 98328
  6.4 0.0 copy-start.5
  6.4 0.9 %copy-done.5 = bf16[128,384]{1,0:T(8,128)(2,1)S(1)} copy-done((bf16[128,384]{1,0:T(8,128)(2,1)S(1)}, bf16[128,384]{1,0:T(8,128)(2,1)}, u32[]{:S(2)}) %copy-start.5) | copy-done | bytes 98328
  7.3 0.0 copy-start.6
  7.3 0.9 %copy-done.6 = bf16[128,384]{1,0:T(8,128)(2,1)S(1)} copy-done((bf16[128,384]{1,0:T(8,128)(2,1)S(1)}, bf16[128,384]{1,0:T(8,128)(2,1)}, u32[]{:S(2)}) %copy-start.6) | copy-done | bytes 98328
  8.2 60.1 %shard_map.82 = bf16[128,640]{1,0:T(8,128)(2,1)S(1)} custom-call(bf16[128,640]{1,0:T(8,128)(2,1)S(1)} %copy-done.1, bf16[128,384]{1,0:T(8,128)(2,1)S(1)} %copy-done.2, bf16[128,384]{1,0:T(8,128)(2,1)S(1)} %copy-done.3, bf16[128,384]{1,0:T(8,128)(2,1)S(1)} %copy-done.4, bf16[128,384]{1,0:T(8,128)(2,1)S(1)} %copy-done.5, bf16[128,384]{1,0:T(8,128)(2,1)S(1)} %copy-done.6, ...), custom_call_target="tpu_custom_call" | custom-call | tf_op jit(solution)/shard_map/pallas_call | solution.py:329
  68.3 0.7 copy.10
Async XLA Ops:
  0.7 2.1 %copy-start = (bf16[384,5120]{1,0:T(8,128)(2,1)S(1)}, bf16[384,5120]{1,0:T(8,128)(2,1)}, u32[]{:S(2)}) copy-start(bf16[384,5120]{1,0:T(8,128)(2,1)} %param.14) | copy-start | bytes 11796484
  2.8 0.9 %copy-start.1 = (bf16[128,640]{1,0:T(8,128)(2,1)S(1)}, bf16[128,640]{1,0:T(8,128)(2,1)}, u32[]{:S(2)}) copy-start(bf16[128,640]{1,0:T(8,128)(2,1)} %hid.1) | copy-start | bytes 491524
  3.7 0.9 %copy-start.2 = (bf16[128,384]{1,0:T(8,128)(2,1)S(1)}, bf16[128,384]{1,0:T(8,128)(2,1)}, u32[]{:S(2)}) copy-start(bf16[128,384]{1,0:T(8,128)(2,1)} %q.1) | copy-start | bytes 294916
  4.6 0.9 %copy-start.3 = (bf16[128,384]{1,0:T(8,128)(2,1)S(1)}, bf16[128,384]{1,0:T(8,128)(2,1)}, u32[]{:S(2)}) copy-start(bf16[128,384]{1,0:T(8,128)(2,1)} %fk.1) | copy-start | bytes 294916
  5.5 0.9 %copy-start.4 = (bf16[128,384]{1,0:T(8,128)(2,1)S(1)}, bf16[128,384]{1,0:T(8,128)(2,1)}, u32[]{:S(2)}) copy-start(bf16[128,384]{1,0:T(8,128)(2,1)} %fv.1) | copy-start | bytes 294916
  6.4 0.9 %copy-start.5 = (bf16[128,384]{1,0:T(8,128)(2,1)S(1)}, bf16[128,384]{1,0:T(8,128)(2,1)}, u32[]{:S(2)}) copy-start(bf16[128,384]{1,0:T(8,128)(2,1)} %sk.1) | copy-start | bytes 294916
  7.3 0.9 %copy-start.6 = (bf16[128,384]{1,0:T(8,128)(2,1)S(1)}, bf16[128,384]{1,0:T(8,128)(2,1)}, u32[]{:S(2)}) copy-start(bf16[128,384]{1,0:T(8,128)(2,1)} %sv.1) | copy-start | bytes 294916

commit v2 on v1

--- a/solution.py
+++ b/solution.py
@@ -316,14 +316,14 @@
     project(2)
     got(yrecv, y_send, y_recv)
     projected = pacc[0] + yrecv[...].astype(F32)
-    mixed = hidv[...].astype(F32) + gatev[...] * projected
+    mixed = hidv[...].astype(F32) + gatev[...][None, :] * projected
     out[...] = mixed.astype(BF16)
     for copy in sent:
         copy.wait_send()
 
 
 def local(hidden_in, queries, fresh_keys, fresh_values, stale_keys, stale_values, out_weight, gate):
-    anywhere = pl.BlockSpec(memory_space=pl.ANY)
+    anywhere = pl.BlockSpec(memory_space=pltpu.HBM)
     vmem, dma = pltpu.VMEM, pltpu.SemaphoreType.DMA
     wide = (HEADS, NY * TOK, 128)
     return pl.pallas_call(
@@ -346,7 +346,7 @@
             vmem((TOK, COLS), BF16),
             vmem((TOK, COLS), BF16),
             vmem((TOK, COLS), BF16),
-            vmem((1, COLS), F32),
+            vmem((COLS,), F32),
             dma((HEADS, 6)),
             dma((2,)),
             dma((2, HEADS, 4)),
@@ -358,11 +358,11 @@
             dma(()),
         ],
         compiler_params=pltpu.CompilerParams(
-            collective_id=0, has_side_effects=True, vmem_limit_bytes=40 * 2**20
+            collective_id=0, has_side_effects=True, vmem_limit_bytes=62 * 2**20
         ),
     )(
         hidden_in, queries, fresh_keys, fresh_values, stale_keys, stale_values,
-        out_weight.reshape(HEADS, TOK, -1), gate.reshape(1, COLS),
+        out_weight.reshape(HEADS, TOK, -1), gate,
     )
 
 

time: 69.3 us -> 62.6 us (0.903)
  local copies, waits for them, and re-layouts: 8.85 us -> 1.6 us
    unnamed x15 -> x1, local copies, waits for them, and re-layouts: 8.16 us -> 1.6 us
where the time goes in v2:
time: 62.6 us; the launch traced here: 62.3 us
  Pallas kernels  60.7 us (97%)
  local copies, waits for them, and re-layouts  1.6 us (3%)
    pallas_call x1, Pallas kernels, local(): pl.pallas_call(kernel, out_shape=jax.ShapeDtypeStruct((TOK, COLS), BF16),...  60.7 us
    unnamed x1, local copies, waits for them, and re-layouts  1.6 us

profile of v2, /device:TPU:56, one launch (start us, length us, event | category | flops | bytes accessed | tf_op | source)
XLA Modules:
  0.0 62.3 jit_solution(12169387241382519278)
XLA Ops:
  0.0 60.7 %shard_map.82 = bf16[128,640]{1,0:T(8,128)(2,1)} custom-call(bf16[128,640]{1,0:T(8,128)(2,1)} %hid.1, bf16[128,384]{1,0:T(8,128)(2,1)} %q.1, bf16[128,384]{1,0:T(8,128)(2,1)} %fk.1, bf16[128,384]{1,0:T(8,128)(2,1)} %fv.1, bf16[128,384]{1,0:T(8,128)(2,1)} %sk.1, bf16[128,384]{1,0:T(8,128)(2,1)} %sv.1, bf16[3,128,5120]{2,1,0:T(8,128)(2,1)} %bitcast.1, f32[640]{0:T(1024)} %gate.1), custom_call_target="tpu_custom_call" | custom-call | tf_op jit(solution)/shard_map/pallas_call | solution.py:329
  60.7 1.6 %copy.10 = bf16[128,640]{1,0:T(8,128)(2,1)} copy(bf16[128,640]{1,0:T(8,128)(2,1)} %shard_map.82) | data formatting | bytes 327680

commit v3 on v2

--- a/solution.py
+++ b/solution.py
@@ -14,12 +14,11 @@
 NY, NZ, NX = 4, 8, 4
 SCALE = 1.4426950408889634 * HEAD_DIM**-0.5
 MESH = pl.DeviceIdType.MESH
+HALF = TOK // 2
+PART = HALF + 16
 F32, BF16 = jnp.float32, jnp.bfloat16
 
-ORDER = (
-    (0, 1), (1, 1), (0, 2), (2, 1), (0, 3), (1, 2),
-    (0, 4), (2, 2), (1, 3), (2, 3), (1, 4), (2, 4),
-)
+ORDER = ((0, 1), (1, 1), (0, 2), (2, 1), (0, 3), (1, 2), (0, 4), (2, 2), (1, 3), (2, 3), (1, 4), (2, 4))
 
 
 def flip(i, k):
@@ -72,6 +71,11 @@
 
     def got(dst, ssem, rsem):
         rc(dst, dst, ssem, rsem, sib).wait_recv()
+
+    barrier = pltpu.get_barrier_semaphore()
+    peers = [zp, zm, sib, *ys[1:], *xs[1:], mate]
+    for peer in peers:
+        pl.semaphore_signal(barrier, inc=1, device_id=peer, device_id_type=MESH)
 
     def cols(h):
         return pl.ds(h * HEAD_DIM, HEAD_DIM)
@@ -98,13 +102,9 @@
         pltpu.make_async_copy(w.at[:, :, own_cols], wb.at[0, :, 0], w_loc.at[0]),
         pltpu.make_async_copy(w.at[:, :, mate_cols], wb.at[1, :, 0], w_loc.at[1]),
     ]
-    for copy in first:
+    for copy in first + later + w_own:
         copy.start()
 
-    barrier = pltpu.get_barrier_semaphore()
-    peers = [zp, zm, sib, *ys[1:], *xs[1:], mate]
-    for peer in peers:
-        pl.semaphore_signal(barrier, inc=1, device_id=peer, device_id_type=MESH)
     for copy in first:
         copy.wait()
     pl.semaphore_wait(barrier, len(peers))
@@ -114,7 +114,7 @@
             return kv.at[h, d, :, 0], kv.at[h, d, :, 1]
         return kv.at[h, 4, 0, 0], kv.at[h, 4, 1, 0]
 
-    def z_start(h, d):
+    def z_start(h, d, way):
         if d == 1:
             src = kv.at[h, 0, :, 0], kv.at[h, 0, :, 0]
         elif d < 4:
@@ -122,8 +122,8 @@
         else:
             src = kv.at[h, 3, 0, 0], kv.at[h, 3, 1, 1]
         dst = z_refs(h, d)
-        for way, to in ((0, zp), (1, zm)):
-            push(src[way], dst[way], z_send.at[way, h, d - 1], z_recv.at[way, h, d - 1], to)
+        to = (zp, zm)[way]
+        push(src[way], dst[way], z_send.at[way, h, d - 1], z_recv.at[way, h, d - 1], to)
 
     def c_refs(h, d):
         if d in (0, 4):
@@ -138,8 +138,8 @@
         dst = z_refs(h, d)
         for way in (0, 1):
             got(dst[way], z_send.at[way, h, d - 1], z_recv.at[way, h, d - 1])
-        if d < 4:
-            z_start(h, d + 1)
+            if d < 4:
+                z_start(h, d + 1, way)
         c_start(h, d)
 
     def q_start(h):
@@ -198,6 +198,13 @@
             for r in (0, 2):
                 attend(h, r, 2, keys, values, False)
 
+    def o_copy(h, k, r):
+        at = pl.ds(r * PART, PART)
+        return (
+            osend.at[h, k - 1, at], orecv.at[h, k - 1, at],
+            o_send.at[r, h, k - 1], o_recv.at[r, h, k - 1],
+        )
+
     def finish(h):
         for k in (1, 2, 3, 0):
             at = pl.ds(k * TOK, TOK)
@@ -208,7 +215,7 @@
                 acc[h, at, :] = o
                 m[h, at, :] = lse
                 continue
-            osend[h, k - 1, pl.ds(0, TOK), :] = o.astype(BF16)
+            o = o.astype(BF16)
             flat = lse.T[:16, :]
             hi = flat.astype(BF16)
             rest = flat - hi.astype(F32)
@@ -217,107 +224,137 @@
             row = lax.broadcasted_iota(jnp.int32, (16, 128), 0)
             three = jnp.where(
                 row == 0, hi.astype(F32), jnp.where(row == 1, mid.astype(F32), low.astype(F32))
-            )
-            osend[h, k - 1, pl.ds(TOK, 16), :] = three.astype(BF16)
-            push(
-                osend.at[h, k - 1], orecv.at[h, k - 1],
-                o_send.at[h, k - 1], o_recv.at[h, k - 1], ys[k],
-            )
-
-    def merge(h):
-        own = pl.ds(0, TOK)
+            ).astype(BF16)
+            for r in (0, 1):
+                osend[h, k - 1, pl.ds(r * PART, HALF), :] = o[r * HALF : (r + 1) * HALF]
+                osend[h, k - 1, pl.ds(r * PART + HALF, 16), :] = three
+            push(*o_copy(h, k, 0), ys[k])
+        for k in (1, 2, 3):
+            push(*o_copy(h, k, 1), ys[k])
+
+    def a_copy(h, k, r):
+        rows = pl.ds(r * HALF, HALF)
+        return (
+            att.at[h, rows], attx.at[h, rows, pl.ds(k * 128, 128)],
+            a_send.at[r, h, k - 1], a_recv.at[r, h, k - 1],
+        )
+
+    def merge(h, r):
+        own = pl.ds(r * HALF, HALF)
         os, lses = [acc[h, own, :]], [m[h, own, :]]
         for k in (1, 2, 3):
-            got(orecv.at[h, k - 1], o_send.at[h, k - 1], o_recv.at[h, k - 1])
-            os.append(orecv[h, k - 1, pl.ds(0, TOK), :].astype(F32))
-            three = orecv[h, k - 1, pl.ds(TOK, 16), :].astype(F32)
+            _, dst, ssem, rsem = o_copy(h, k, r)
+            got(dst, ssem, rsem)
+            os.append(orecv[h, k - 1, pl.ds(r * PART, HALF), :].astype(F32))
+            three = orecv[h, k - 1, pl.ds(r * PART + HALF, 16), :].astype(F32)
             flat = three[0:1] + three[1:2] + three[2:3]
-            lses.append(jnp.broadcast_to(flat, (TOK, 128)).T)
+            lses.append(jnp.broadcast_to(flat, (TOK, 128)).T[r * HALF : (r + 1) * HALF])
         top = functools.reduce(jnp.maximum, lses)
         ws = [jnp.exp2(e - top) for e in lses]
         den = functools.reduce(jnp.add, ws)
         num = functools.reduce(jnp.add, [a * b for a, b in zip(ws, os, strict=True)])
         result = (num / den).astype(BF16)
-        att[h] = result
-        attx[h, :, pl.ds(0, 128)] = result
-        for k in (1, 2, 3):
-            push(
-                att.at[h], attx.at[h, :, pl.ds(k * 128, 128)],
-                a_send.at[h, k - 1], a_recv.at[h, k - 1], xs[k],
-            )
+        att[h, own, :] = result
+        attx[h, own, pl.ds(0, 128)] = result
+        for k in (1, 2, 3):
+            push(*a_copy(h, k, r), xs[k])
+
+    def await_att(h, r):
+        for k in (1, 2, 3):
+            _, dst, ssem, rsem = a_copy(h, k, r)
+            got(dst, ssem, rsem)
+
+    def await_w(h):
+        for k in (1, 2, 3):
+            got(wb.at[1 - c, h, k], wc_send.at[h, k - 1], wc_recv.at[h, k - 1])
+
+    def weights(part, h):
+        return wb[part, h].reshape(NX * TOK, COLS)
 
     def project(h):
-        for k in (1, 2, 3):
-            got(attx.at[h, :, pl.ds(k * 128, 128)], a_send.at[h, k - 1], a_recv.at[h, k - 1])
-            got(wb.at[1 - c, h, k], wc_send.at[h, k - 1], wc_recv.at[h, k - 1])
-        a = attx[h]
+        await_w(h)
+        await_att(h, 0)
+        await_att(h, 1)
         for part in (1, 0):
-            term = dot(a, wb[part, h].reshape(NX * TOK, COLS))
-            if h > 0:
-                term = pacc[part] + term
-            if h < HEADS - 1 or part == 0:
-                pacc[part] = term
-            else:
-                ysend[...] = term.astype(BF16)
-                push(ysend, yrecv, y_send, y_recv, mate)
-
-    z_start(0, 1)
-    q_start(0)
-    z_start(1, 1)
+            term = dot(attx[h], weights(part, h))
+            pacc[part] = pacc[part] + term if h > 0 else term
+
+    def y_copy(r):
+        rows = pl.ds(r * HALF, HALF)
+        return ysend.at[rows], yrecv.at[rows], y_send.at[r], y_recv.at[r]
+
+    def project_last():
+        h = HEADS - 1
+        await_w(h)
+        for r in (0, 1):
+            rows = pl.ds(r * HALF, HALF)
+            await_att(h, r)
+            term = pacc[1, rows, :] + dot(attx[h, rows, :], weights(1, h))
+            ysend[rows, :] = term.astype(BF16)
+            push(*y_copy(r), mate)
+        pacc[0] = pacc[0] + dot(attx[h], weights(0, h))
+
+    for h in range(HEADS):
+        z_start(h, 1, 0)
+        z_start(h, 1, 1)
+        q_start(h)
     for h in range(HEADS):
         c_start(h, 0)
-    q_start(1)
-    z_start(2, 1)
-    q_start(2)
-    for copy in later:
-        copy.start()
     for h in range(HEADS):
         w_start(h)
-    for copy in w_own:
-        copy.start()
     for copy in later:
         copy.wait()
-
-    todo = {i: [] for i in range(len(ORDER) + 1)}
-    todo[1].append((0, 0))
-    todo[2].append((0, 1))
-    todo[3].append((1, 0))
-    todo[4].append((1, 1))
-    todo[5].append((0, 2))
-    todo[6].append((2, 0))
-    todo[7].append((0, 3))
-    todo[7].append((2, 1))
-    todo[8].append((0, 4))
-    todo[8].append((1, 2))
-    todo[9].append((2, 2))
-    todo[10].append((1, 3))
-    todo[11].append((2, 3))
-    todo[11].append((1, 4))
-    todo[12].append((2, 4))
-    for i in range(len(ORDER) + 1):
-        if i < len(ORDER):
-            relay(*ORDER[i])
-        for h, d in todo[i]:
-            work(h, d)
-            if d == 4:
-                finish(h)
-        if i == 9:
-            w_relay(0)
-        if i == 11:
-            merge(0)
+    relay(0, 1)
+    work(0, 0)
+    relay(1, 1)
+    work(0, 1)
+    relay(0, 2)
+    work(1, 0)
+    work(1, 1)
+    relay(2, 1)
+    work(0, 2)
+    relay(0, 3)
+    work(2, 0)
+    work(2, 1)
+    relay(1, 2)
+    relay(0, 4)
+    work(0, 3)
+    w_relay(0)
+    relay(2, 2)
+    work(1, 2)
+    work(0, 4)
+    finish(0)
+    relay(1, 3)
+    work(2, 2)
+    relay(2, 3)
+    relay(1, 4)
+    work(1, 3)
     w_relay(1)
-    merge(1)
+    relay(2, 4)
+    work(2, 3)
+    merge(0, 0)
+    merge(0, 1)
+    work(1, 4)
+    finish(1)
+    work(2, 4)
+    finish(2)
+    w_relay(2)
+    merge(1, 0)
+    merge(1, 1)
+    merge(2, 0)
+    merge(2, 1)
     for copy in w_own:
         copy.wait()
     project(0)
-    merge(2)
-    w_relay(2)
     project(1)
-    project(2)
-    got(yrecv, y_send, y_recv)
-    projected = pacc[0] + yrecv[...].astype(F32)
-    mixed = hidv[...].astype(F32) + gatev[...][None, :] * projected
-    out[...] = mixed.astype(BF16)
+    project_last()
+    for r in (0, 1):
+        rows = pl.ds(r * HALF, HALF)
+        _, dst, ssem, rsem = y_copy(r)
+        got(dst, ssem, rsem)
+        projected = pacc[0, rows, :] + yrecv[rows, :].astype(F32)
+        mixed = hidv[rows, :].astype(F32) + gatev[...][None, :] * projected
+        out[rows, :] = mixed.astype(BF16)
     for copy in sent:
         copy.wait_send()
 
@@ -337,8 +374,8 @@
             vmem(wide, F32),
             vmem(wide, F32),
             vmem(wide, F32),
-            vmem((HEADS, 3, TOK + 16, 128), BF16),
-            vmem((HEADS, 3, TOK + 16, 128), BF16),
+            vmem((HEADS, 3, 2 * PART, 128), BF16),
+            vmem((HEADS, 3, 2 * PART, 128), BF16),
             vmem((HEADS, TOK, 128), BF16),
             vmem((HEADS, TOK, NX * 128), BF16),
             vmem((2, HEADS, NX, TOK, COLS), BF16),
@@ -353,9 +390,11 @@
             dma((2, HEADS, 4)),
             dma((HEADS, 5)),
             dma((HEADS, 5)),
-            *[dma((HEADS, 3)) for _ in range(10)],
-            dma(()),
-            dma(()),
+            *[dma((HEADS, 3)) for _ in range(2)],
+            *[dma((2, HEADS, 3)) for _ in range(4)],
+            *[dma((HEADS, 3)) for _ in range(4)],
+            dma((2,)),
+            dma((2,)),
         ],
         compiler_params=pltpu.CompilerParams(
             collective_id=0, has_side_effects=True, vmem_limit_bytes=62 * 2**20

time: 62.6 us -> 62.6 us (level)
  no operation moved by 1% of the time
where the time goes in v3:
time: 62.6 us; the launch traced here: 62.2 us
  Pallas kernels  60.6 us (97%)
  local copies, waits for them, and re-layouts  1.6 us (3%)
    pallas_call x1, Pallas kernels, local(): pl.pallas_call(kernel, out_shape=jax.ShapeDtypeStruct((TOK, COLS), BF16),...  60.6 us
    unnamed x1, local copies, waits for them, and re-layouts  1.6 us

profile of v3, /device:TPU:56, one launch (start us, length us, event | category | flops | bytes accessed | tf_op | source)
XLA Modules:
  0.0 62.2 jit_solution(2404299975882117982)
XLA Ops:
  0.0 60.6 %shard_map.82 = bf16[128,640]{1,0:T(8,128)(2,1)} custom-call(bf16[128,640]{1,0:T(8,128)(2,1)} %hid.1, bf16[128,384]{1,0:T(8,128)(2,1)} %q.1, bf16[128,384]{1,0:T(8,128)(2,1)} %fk.1, bf16[128,384]{1,0:T(8,128)(2,1)} %fv.1, bf16[128,384]{1,0:T(8,128)(2,1)} %sk.1, bf16[128,384]{1,0:T(8,128)(2,1)} %sv.1, bf16[3,128,5120]{2,1,0:T(8,128)(2,1)} %bitcast.1, f32[640]{0:T(1024)} %gate.1), custom_call_target="tpu_custom_call" | custom-call | tf_op jit(solution)/shard_map/pallas_call | solution.py:366
  60.6 1.6 %copy.10 = bf16[128,640]{1,0:T(8,128)(2,1)} copy(bf16[128,640]{1,0:T(8,128)(2,1)} %shard_map.82) | data formatting | bytes 327680
